TPU v7x, 32 devices: a whole 2x2x4 slice. The times are simulated.
32 devices in a mesh: row: 8 (over z, x), col: 2 (over y), rep: 2 (over core).
Axes of the slice: x: 2, y: 2, z: 4, core: 2. Of those that a mesh axis runs over, the one named last changes fastest.
Arguments:
- basis: bfloat16 [64, 1024, 128], P('row', None, 'rep'), may hold values from -6 to 6
- tiles: bfloat16 [8, 2, 4, 1024, 1024], P('row', 'col'), may hold values from -1.5 to 1.5
- slots: int32 [8, 2, 4, 2], P('row', 'col'), may hold values from -1 to 63, as said below
- sectors: int32 [64, 1024], replicated, may hold values from 0 to 10
Outputs:
- next_basis: float32 [64, 1024, 128], P('row', 'col', 'rep')
- projected: float32 [2, 128, 128], replicated
Inputs may be any that keep to these rules, and one draw needn't show every extreme that they name: For owner (r, c), the first two indices of slots, each live slot holds (I, J) with 8 * r <= I < 8 * (r + 1) and 32 * c <= J < 32 * (c + 1). Live slots come first, every owner has at least one, an empty slot holds (-1, -1). Each pair of block indices, in either order, is held by one live slot at most among all owners. At most 4 live slots an owner, and some owner has all 4 live.
All inputs are finite; a program needn't handle non-finite values.
Results may differ from a plain program's by a relative error of at most 0.0025.
Values may be sent and summed in bfloat16 or wider, within the bound.
A program may use at most 128 MiB of HBM per device.

v0:
```python
import jax
import jax.numpy as jnp
from jax import lax
from jax.sharding import PartitionSpec as P

PRODUCTS = 2


def projections(own_rows, previous, widened, rep_index, total_rows, full_cols):
    gram_block = jnp.dot(own_rows.T, widened, precision=lax.Precision.HIGHEST) / total_rows
    ritz_block = (
        jnp.dot(previous.astype(jnp.float32).T, widened, precision=lax.Precision.HIGHEST)
        / total_rows
    )
    zero_matrix = jnp.zeros((full_cols, full_cols), jnp.float32)
    row_start = rep_index * own_rows.shape[1]
    gram_part = lax.dynamic_update_slice_in_dim(zero_matrix, gram_block, row_start, 0)
    ritz_part = lax.dynamic_update_slice_in_dim(zero_matrix, ritz_block, row_start, 0)
    return (gram_part, ritz_part)


def solve_rows(gram_matrix, widened):
    factor = jnp.linalg.cholesky(gram_matrix)
    return jax.scipy.linalg.solve_triangular(factor, widened.T, lower=True).T


def body(basis, tiles, slots, sectors):
    row_count = lax.axis_size("row")
    col_count = lax.axis_size("col")
    row_index = lax.axis_index("row")
    col_index = lax.axis_index("col")
    rep_index = lax.axis_index("rep")
    blocks_here, tile_width, half_cols = basis.shape
    group_size = row_count // col_count
    col_blocks = blocks_here * group_size
    share_rows = tile_width // col_count
    total_rows = blocks_here * row_count * tile_width
    full_cols = half_cols * lax.axis_size("rep")
    slot_pairs = slots.reshape(-1, 2)
    tile_stack = tiles.reshape(-1, tile_width, tile_width)
    live_count = jnp.sum((slot_pairs[:, 0] >= 0).astype(jnp.int32))
    block_rows = jnp.maximum(slot_pairs[:, 0], 0)
    block_cols = jnp.maximum(slot_pairs[:, 1], 0)
    local_rows = jnp.clip(block_rows - blocks_here * row_index, 0, blocks_here - 1)
    local_cols = jnp.clip(block_cols - col_blocks * col_index, 0, col_blocks - 1)
    same_sector = sectors[block_rows][:, :, None] == sectors[block_cols][:, None, :]
    masked = jnp.where(same_sector, tile_stack, jnp.zeros((), tile_stack.dtype))
    row_panel = basis
    outcome = None
    history = []
    for rounds in range(PRODUCTS):
        whole_panel = lax.all_gather(row_panel, "row", axis=0, tiled=True)
        columns = lax.dynamic_slice_in_dim(whole_panel, col_index * col_blocks, col_blocks, 0)

        def accumulate(position, partials, columns=columns, row_panel=row_panel):
            row_totals, col_totals = partials
            one_tile = lax.dynamic_index_in_dim(masked, position, 0, keepdims=False)
            row_slot = local_rows[position]
            col_slot = local_cols[position]
            col_input = lax.dynamic_index_in_dim(columns, col_slot, 0, keepdims=False)
            row_input = lax.dynamic_index_in_dim(row_panel, row_slot, 0, keepdims=False)
            forward = jnp.dot(one_tile, col_input, preferred_element_type=jnp.float32)
            backward = lax.dot_general(
                one_tile, row_input, (((0,), (0,)), ((), ())), preferred_element_type=jnp.float32
            )
            return (row_totals.at[row_slot].add(forward), col_totals.at[col_slot].add(backward))

        initial = (jnp.zeros(row_panel.shape, jnp.float32), jnp.zeros(columns.shape, jnp.float32))
        row_part, col_part = lax.fori_loop(0, live_count, accumulate, initial)
        col_share = lax.psum_scatter(col_part, "row", scatter_dimension=1, tiled=True)
        col_total = lax.all_gather(col_share, "row", axis=1, tiled=True)
        own_block = lax.dynamic_slice_in_dim(
            col_total, row_index % group_size * blocks_here, blocks_here, 0
        )
        is_owner = row_index // group_size == col_index
        row_part = row_part + jnp.where(is_owner, own_block, jnp.zeros_like(own_block))
        summed = lax.psum(row_part, "col")
        own_rows = summed.reshape(-1, half_cols)
        previous = row_panel.reshape(-1, half_cols)
        widened = lax.all_gather(own_rows, "rep", axis=1, tiled=True)
        gram_part, ritz_part = projections(
            own_rows, previous, widened, rep_index, total_rows, full_cols
        )
        gram_matrix, ritz_matrix = lax.psum((gram_part, ritz_part), ("row", "rep"))
        solved = solve_rows(gram_matrix, widened)
        chosen = lax.dynamic_slice_in_dim(solved, rep_index * half_cols, half_cols, 1)
        next_block = chosen.reshape(blocks_here, tile_width, half_cols)
        outcome = lax.dynamic_slice_in_dim(next_block, col_index * share_rows, share_rows, 1)
        row_panel = lax.optimization_barrier(next_block.astype(jnp.bfloat16))
        history.append(ritz_matrix)
    return (outcome, jnp.stack(history))


def solution(mesh):
    placed = (
        P("row", None, "rep"),
        P("row", "col", None, None, None),
        P("row", "col", None, None),
        P(),
    )
    return jax.shard_map(
        body, mesh=mesh, in_specs=placed, out_specs=(P("row", "col", "rep"), P()), check_vma=False
    )
```

profile of v0, /device:TPU:0, one launch (start us, length us, event | category | flops | bytes accessed | tf_op | source)
XLA Modules:
  0.0 1371.9 jit_solution(6657256790378834700)
XLA Ops:
  10.6 7.8 compare_select_fusion
  18.4 119.4 %all-gather.7.cloned.1.call-done = bf16[64,1024,64]{1,2,0:T(8,128)(2,1)} async-done(((bf16[8,1024,64]{1,2,0:T(8,128)(2,1)}), bf16[64,1024,64]{1,2,0:T(8,128)(2,1)}) %all-gather.7.cloned.1.call-update) | async-done | bytes 8388624 | tf_op jit(solution)/shard_map/all_gather | solution.py:52
  147.2 13.8 %while.28 = (s32[]{:T(128)}, f32[8,1024,64]{1,2,0:T(8,128)S(1)}, f32[32,1024,64]{1,2,0:T(8,128)}, s32[]{:T(128)}, s32[4]{0:T(128)S(1)}, /*index=5*/bf16[4,1024,1...) while((s32[]{:T(128)}, f32[8,1024,64]{1,2,0:T(8,128)S(1)}, ...), condition=%wide.region_4.5_spmd, body=%wide.region_1.4_spmd.sunk | while | flops 268697664 | bytes 5508433 | solution.py:69
  161.1 186.9 %reduce-scatter.3.cloned.1.call-done = f32[32,128,64]{1,2,0:T(8,128)} async-done(((f32[32,1024,64]{1,2,0:T(8,128)}), f32[32,128,64]{1,2,0:T(8,128)}) %reduce-scatter.3.cloned.1.call-update) | async-done | bytes 1048592 | tf_op jit(solution)/shard_map/reduce_scatter | solution.py:70
  348.0 126.6 %all-gather.9.cloned.1.call-done = f32[32,1024,64]{1,2,0:T(8,128)} async-done(((f32[32,128,64]{1,2,0:T(8,128)}), f32[32,1024,64]{1,2,0:T(8,128)}) %all-gather.9.cloned.1.call-update) | async-done | bytes 8388624 | tf_op jit(solution)/shard_map/all_gather | solution.py:71
  478.2 61.2 %all-reduce.6.cloned.1.call-done = f32[8192,64]{0,1:T(8,128)} async-done(((f32[8192,64]{0,1:T(8,128)}), f32[8192,64]{0,1:T(8,128)}) %all-reduce.6.cloned.1.call-update) | async-done | bytes 2097168 | tf_op jit(solution)/shard_map/psum | solution.py:77
  539.5 15.0 %all-gather.11.cloned.1.call-done = f32[8192,128]{0,1:T(8,128)} async-done(((f32[8192,64]{0,1:T(8,128)}), f32[8192,128]{0,1:T(8,128)}) %all-gather.11.cloned.1.call-update) | async-done | bytes 4194320 | tf_op jit(solution)/shard_map/all_gather | solution.py:80
  554.5 5.9 convolution_multiply_fusion.2
  562.0 85.4 %all-reduce.8.cloned.1.call-done = f32[128,128]{0,1:T(8,128)} async-done(((f32[128,128]{0,1:T(8,128)}), f32[128,128]{0,1:T(8,128)}) %all-reduce.8.cloned.1.call-update) | async-done | bytes 65552 | tf_op jit(solution)/shard_map/psum | solution.py:84
  649.2 11.7 cholesky.44
  662.2 9.8 custom-call.6
  672.1 6.0 fusion.73
  680.6 126.5 %all-gather.13.cloned.1.call-done = bf16[64,1024,64]{1,2,0:T(8,128)(2,1)} async-done(((bf16[8,1024,64]{1,2,0:T(8,128)(2,1)}), bf16[64,1024,64]{1,2,0:T(8,128)(2,1)}) %all-gather.13.cloned.1.call-update) | async-done | bytes 8388624 | tf_op jit(solution)/shard_map/all_gather | solution.py:52
  807.0 4.9 constant_dynamic-slice_fusion.3
  816.5 14.8 %while.29 = (s32[]{:T(128)}, f32[8,1024,64]{1,2,0:T(8,128)S(1)}, f32[32,1024,64]{1,2,0:T(8,128)}, s32[]{:T(128)}, s32[4]{0:T(128)S(1)}, /*index=5*/bf16[4,1024,1...) while((s32[]{:T(128)}, f32[8,1024,64]{1,2,0:T(8,128)S(1)}, ...), condition=%wide.region_13.16_spmd, body=%wide.region_10.15_spmd.sunk | while | flops 268697664 | bytes 6163285 | solution.py:69
  831.3 189.9 %reduce-scatter.5.cloned.1.call-done = f32[32,128,64]{1,2,0:T(8,128)} async-done(((f32[32,1024,64]{1,2,0:T(8,128)}), f32[32,128,64]{1,2,0:T(8,128)}) %reduce-scatter.5.cloned.1.call-update) | async-done | bytes 1048592 | tf_op jit(solution)/shard_map/reduce_scatter | solution.py:70
  1021.3 126.4 %all-gather.15.cloned.1.call-done = f32[32,1024,64]{1,2,0:T(8,128)} async-done(((f32[32,128,64]{1,2,0:T(8,128)}), f32[32,1024,64]{1,2,0:T(8,128)}) %all-gather.15.cloned.1.call-update) | async-done | bytes 8388624 | tf_op jit(solution)/shard_map/all_gather | solution.py:71
  1151.3 61.2 %all-reduce.10.cloned.1.call-done = f32[8192,64]{0,1:T(8,128)} async-done(((f32[8192,64]{0,1:T(8,128)}), f32[8192,64]{0,1:T(8,128)}) %all-reduce.10.cloned.1.call-update) | async-done | bytes 2097168 | tf_op jit(solution)/shard_map/psum | solution.py:77
  1219.0 8.8 all-gather.17.cloned.1.call-done
  1232.4 5.5 convolution_multiply_fusion.1
  1239.0 91.9 %all-reduce.12.cloned.1.call-done = (f32[128,128]{0,1:T(8,128)}, f32[1,128,128]{2,1,0:T(8,128)}, f32[1,128,128]{2,1,0:T(8,128)}) async-done(((f32[128,128]{0,1:T(8,128)}, f32[1,128,128]{2,1,0:T(8,128)}, f32[1,128,128]{2,1,0:T(8,128)}), (f32[128,128]{0,1:T(8,128)}, f32[1,128,128]{2,1,0:T(8,128)}, f32[1,128,128]{2,1,0:T(8,128)})) %all-reduce.12.cloned.1.call-update) | async-done | bytes 196624 | tf_op jit(solution)/shard_map/psum | solution.py:84
  1332.7 11.7 cholesky.55
  1345.8 9.8 custom-call.7
  1355.6 5.5 fusion.71
  (103 shorter events, 68.7 us)
Async XLA Ops:
  7.2 2.3 copy-start
  7.2 130.6 %all-gather.7.cloned.1.call-start = ((), (), s32[]{:S(2)}) async-start(), calls=%async_computation.2 | async-start | bytes 9437184 | tf_op jit(solution)/shard_map/all_gather | solution.py:52
  7.9 340.0 %reduce-scatter.3.cloned.1.call-start = ((), (), s32[]{:S(2)}) async-start(), calls=%async_computation.3 | async-start | bytes 9437184 | tf_op jit(solution)/shard_map/reduce_scatter | solution.py:70
  142.9 4.3 copy-start.10
  142.9 4.3 copy-start.11
  161.0 313.6 %all-gather.9.cloned.1.call-start = ((), (), s32[]{:S(2)}) async-start(), calls=%async_computation.4 | async-start | bytes 9437184 | tf_op jit(solution)/shard_map/all_gather | solution.py:71
  348.0 191.4 %all-reduce.6.cloned.1.call-start = ((), (), s32[]{:S(2)}) async-start(), calls=%async_computation.5 | async-start | bytes 4194304 | tf_op jit(solution)/shard_map/psum | solution.py:77
  478.1 76.4 %all-gather.11.cloned.1.call-start = ((), (), s32[]{:S(2)}) async-start(), calls=%async_computation.6 | async-start | bytes 6291456 | tf_op jit(solution)/shard_map/all_gather | solution.py:80
  539.4 108.0 %all-reduce.8.cloned.1.call-start = ((), (), s32[]{:S(2)}) async-start(), calls=%async_computation.7 | async-start | bytes 131072 | tf_op jit(solution)/shard_map/psum | solution.py:84
  560.8 0.6 copy-start.7
  561.5 245.6 %all-gather.13.cloned.1.call-start = ((), (), s32[]{:S(2)}) async-start(), calls=%async_computation.8 | async-start | bytes 9437184 | tf_op jit(solution)/shard_map/all_gather | solution.py:52
  680.4 340.9 %reduce-scatter.5.cloned.1.call-start = ((), (), s32[]{:S(2)}) async-start(), calls=%async_computation.9 | async-start | bytes 9437184 | tf_op jit(solution)/shard_map/reduce_scatter | solution.py:70
  831.3 316.4 %all-gather.15.cloned.1.call-start = ((), (), s32[]{:S(2)}) async-start(), calls=%async_computation.10 | async-start | bytes 9437184 | tf_op jit(solution)/shard_map/all_gather | solution.py:71
  1021.2 191.2 %all-reduce.10.cloned.1.call-start = ((), (), s32[]{:S(2)}) async-start(), calls=%async_computation.11 | async-start | bytes 4194304 | tf_op jit(solution)/shard_map/psum | solution.py:77
  1149.7 62.8 %copy-start.3 = (bf16[8,1024,64]{1,2,0:T(8,128)(2,1)S(1)}, bf16[8,1024,64]{1,2,0:T(8,128)(2,1)}, u32[]{:S(2)}) copy-start(bf16[8,1024,64]{1,2,0:T(8,128)(2,1)} %get-tuple-element.499) | copy-start | bytes 3145732
  1151.2 76.6 %all-gather.17.cloned.1.call-start = ((), (), s32[]{:S(2)}) async-start(), calls=%async_computation.12 | async-start | bytes 6291456 | tf_op jit(solution)/shard_map/all_gather | solution.py:80
  1212.5 118.4 %all-reduce.12.cloned.1.call-start = ((), (), s32[]{:S(2)}) async-start(), calls=%async_computation.13 | async-start | bytes 393216 | tf_op jit(solution)/shard_map/psum | solution.py:84
  1217.4 20.5 %copy-start.4 = (f32[1,128,128]{2,1,0:T(8,128)}, f32[1,128,128]{2,1,0:T(8,128)S(1)}, u32[]{:S(2)}) copy-start(f32[1,128,128]{2,1,0:T(8,128)S(1)} %fusion.77) | copy-start | bytes 196612
  1217.4 15.0 %copy-start.2 = (f32[8192,64]{0,1:T(8,128)S(1)}, f32[8192,64]{0,1:T(8,128)}, u32[]{:S(2)}) copy-start(f32[8192,64]{0,1:T(8,128)} %all-reduce.10.cloned.1.call-done) | copy-start | bytes 6291460
  1238.3 0.6 copy-start.6
  1238.4 0.6 copy-start.5
  1361.2 3.7 copy-start.1
  1361.2 3.0 copy-start.8
  1361.2 3.0 copy-start.9
Sparse Core Ops, SparseCore 0:
  10.1 127.6 all-gather.6
  161.2 186.7 reduce-scatter.2
  350.2 124.3 all-gather.8
  478.2 61.0 all-reduce.5
  540.8 13.6 all-gather.10
  561.6 85.7 all-reduce.7
  680.5 126.5 all-gather.12
  831.4 189.7 reduce-scatter.4
  1023.3 124.3 all-gather.14
  1151.3 61.0 all-reduce.9
  1214.1 13.6 all-gather.16
  1239.1 91.7 all-reduce.11
where the time goes:
time: 1380 us; the launch traced here: 1370 us
  waiting for transfers between devices  1200 us (87%)
  other arithmetic  62.9 us (5%)
  matrix products  44.9 us (3%)
  local copies, waits for them, and re-layouts  37.5 us (3%)
  between operations  14.8 us (1%)
    reduce_scatter x2, waiting for transfers between devices, body(): lax.psum_scatter(col_part, 'row', scatter_dimension=1, tiled=True)  377 us
    all_gather x2, waiting for transfers between devices, body(): col_total = lax.all_gather(col_share, 'row', axis=1, tiled=True)  253 us
    all_gather x2, waiting for transfers between devices, body(): whole_panel = lax.all_gather(row_panel, 'row', axis=0, tiled=True)  246 us
    psum x2, waiting for transfers between devices, body(): gram_matrix, ritz_matrix = lax.psum((gram_part, ritz_part), ('row', 'rep'))  177 us
    psum x2, waiting for transfers between devices, body(): summed = lax.psum(row_part, 'col')  122 us
  transfers between devices with their start and end apart: 12, of which 12 were waited for; matrix products, arithmetic and copies ran while one was open for 1% of the time, Pallas kernels for 0%

commit v1 on v0

--- a/solution.py
+++ b/solution.py
@@ -68,7 +68,17 @@
         initial = (jnp.zeros(row_panel.shape, jnp.float32), jnp.zeros(columns.shape, jnp.float32))
         row_part, col_part = lax.fori_loop(0, live_count, accumulate, initial)
         col_share = lax.psum_scatter(col_part, "row", scatter_dimension=1, tiled=True)
-        col_total = lax.all_gather(col_share, "row", axis=1, tiled=True)
+        even = lax.axis_size("row")
+        b_now, local_part = (even, lax.axis_index("row"))
+        col_total, right_arr = (col_share, 1)
+        while right_arr < b_now:
+            v_now = lax.ppermute(
+                col_total, "row", [(src_i, src_i ^ right_arr) for src_i in range(b_now)]
+            )
+            z1 = jnp.concatenate([col_total, v_now], axis=1)
+            lower = jnp.concatenate([v_now, col_total], axis=1)
+            col_total = jnp.where(local_part & right_arr == 0, z1, lower)
+            right_arr = 2 * right_arr
         own_block = lax.dynamic_slice_in_dim(
             col_total, row_index % group_size * blocks_here, blocks_here, 0
         )

time: 1380 us -> 1650 us (1.20)
  waiting for transfers between devices: 1200 us -> 1450 us
    ppermute x0 -> x6, waiting for transfers between devices: none -> 501 us  [body(): lax.ppermute(col_total, 'row', [(src_i, src_i ^ right_arr) for src_i in r...]
    all_gather x2 -> x0, waiting for transfers between devices: 253 us -> none  [body(): col_total = lax.all_gather(col_share, 'row', axis=1, tiled=True)]
  transfers between devices with their start and end apart: 12 -> 16, of which waited for: 12 -> 16; matrix products, arithmetic and copies ran while one was open for 1% -> 1% of each run, Pallas kernels for 0% -> 0%
where the time goes in v1:
time: 1650 us; the launch traced here: 1640 us
  waiting for transfers between devices  1450 us (88%)
  other arithmetic  74.7 us (5%)
  matrix products  44.9 us (3%)
  local copies, waits for them, and re-layouts  37.7 us (2%)
    ppermute x6, waiting for transfers between devices, body(): lax.ppermute(col_total, 'row', [(src_i, src_i ^ right_arr) for src_i in r...  501 us
    reduce_scatter x2, waiting for transfers between devices, body(): lax.psum_scatter(col_part, 'row', scatter_dimension=1, tiled=True)  377 us
    all_gather x2, waiting for transfers between devices, body(): whole_panel = lax.all_gather(row_panel, 'row', axis=0, tiled=True)  246 us
    psum x2, waiting for transfers between devices, body(): gram_matrix, ritz_matrix = lax.psum((gram_part, ritz_part), ('row', 'rep'))  177 us
    psum x2, waiting for transfers between devices, body(): summed = lax.psum(row_part, 'col')  125 us
  transfers between devices with their start and end apart: 16, of which 16 were waited for; matrix products, arithmetic and copies ran while one was open for 1% of the time, Pallas kernels for 0%

profile of v1, /device:TPU:0, one launch (start us, length us, event | category | flops | bytes accessed | tf_op | source)
XLA Modules:
  0.0 1640.7 jit_solution(95200692921155857)
XLA Ops:
  10.6 7.8 compare_select_fusion
  18.4 119.4 %all-gather.5.cloned.1.call-done = bf16[64,1024,64]{1,2,0:T(8,128)(2,1)} async-done(((bf16[8,1024,64]{1,2,0:T(8,128)(2,1)}), bf16[64,1024,64]{1,2,0:T(8,128)(2,1)}) %all-gather.5.cloned.1.call-update) | async-done | bytes 8388624 | tf_op jit(solution)/shard_map/all_gather | solution.py:52
  147.2 13.8 while.28
  161.1 186.9 %reduce-scatter.3.cloned.1.call-done = f32[32,128,64]{1,2,0:T(8,128)} async-done(((f32[32,1024,64]{1,2,0:T(8,128)}), f32[32,128,64]{1,2,0:T(8,128)}) %reduce-scatter.3.cloned.1.call-update) | async-done | bytes 1048592 | tf_op jit(solution)/shard_map/reduce_scatter | solution.py:70
  349.4 23.7 %collective-permute-done = f32[32,128,64]{1,2,0:T(8,128)S(1)} collective-permute-done((f32[32,128,64]{1,2,0:T(8,128)}, f32[32,128,64]{1,2,0:T(8,128)S(1)}, u32[]{:S(2)}, u32[]{:S(2)}) %collective-permute-start) | collective-permute-done | bytes 1048608 | tf_op jit(solution)/shard_map/ppermute | solution.py:75
  376.3 46.9 %collective-permute-done.1 = f32[32,256,64]{1,2,0:T(8,128)} collective-permute-done((f32[32,256,64]{1,2,0:T(8,128)}, f32[32,256,64]{1,2,0:T(8,128)}, u32[]{:S(2)}, u32[]{:S(2)}) %collective-permute-start.1) | collective-permute-done | bytes 2097184 | tf_op jit(solution)/shard_map/ppermute | solution.py:75
  423.2 6.5 maximum_select_fusion
  430.9 180.5 %collective-permute-done.2 = f32[32,512,64]{1,2,0:T(8,128)} collective-permute-done((f32[32,512,64]{1,2,0:T(8,128)}, f32[32,512,64]{1,2,0:T(8,128)}, u32[]{:S(2)}, u32[]{:S(2)}) %collective-permute-start.2) | collective-permute-done | bytes 4194336 | tf_op jit(solution)/shard_map/ppermute | solution.py:75
  615.9 62.7 %all-reduce.6.cloned.1.call-done = f32[8192,64]{0,1:T(8,128)} async-done(((f32[8192,64]{0,1:T(8,128)}), f32[8192,64]{0,1:T(8,128)}) %all-reduce.6.cloned.1.call-update) | async-done | bytes 2097168 | tf_op jit(solution)/shard_map/psum | solution.py:87
  678.7 15.0 all-gather.7.cloned.1.call-done
  701.2 85.4 %all-reduce.8.cloned.1.call-done = f32[128,128]{0,1:T(8,128)} async-done(((f32[128,128]{0,1:T(8,128)}), f32[128,128]{0,1:T(8,128)}) %all-reduce.8.cloned.1.call-update) | async-done | bytes 65552 | tf_op jit(solution)/shard_map/psum | solution.py:94
  788.4 11.7 cholesky.44
  801.5 9.8 custom-call.6
  819.8 126.5 %all-gather.9.cloned.1.call-done = bf16[64,1024,64]{1,2,0:T(8,128)(2,1)} async-done(((bf16[8,1024,64]{1,2,0:T(8,128)(2,1)}), bf16[64,1024,64]{1,2,0:T(8,128)(2,1)}) %all-gather.9.cloned.1.call-update) | async-done | bytes 8388624 | tf_op jit(solution)/shard_map/all_gather | solution.py:52
  955.7 14.8 while.29
  970.5 189.9 %reduce-scatter.5.cloned.1.call-done = f32[32,128,64]{1,2,0:T(8,128)} async-done(((f32[32,1024,64]{1,2,0:T(8,128)}), f32[32,128,64]{1,2,0:T(8,128)}) %reduce-scatter.5.cloned.1.call-update) | async-done | bytes 1048592 | tf_op jit(solution)/shard_map/reduce_scatter | solution.py:70
  1161.9 23.7 %collective-permute-done.3 = f32[32,128,64]{1,2,0:T(8,128)S(1)} collective-permute-done((f32[32,128,64]{1,2,0:T(8,128)}, f32[32,128,64]{1,2,0:T(8,128)S(1)}, u32[]{:S(2)}, u32[]{:S(2)}) %collective-permute-start.3) | collective-permute-done | bytes 1048608 | tf_op jit(solution)/shard_map/ppermute | solution.py:75
  1187.5 46.6 %collective-permute-done.4 = f32[32,256,64]{1,2,0:T(8,128)S(1)} collective-permute-done((f32[32,256,64]{1,2,0:T(8,128)S(1)}, f32[32,256,64]{1,2,0:T(8,128)S(1)}, u32[]{:S(2)}, u32[]{:S(2)}) %collective-permute-start.4) | collective-permute-done | bytes 2097184 | tf_op jit(solution)/shard_map/ppermute | solution.py:75
  1236.2 180.1 %collective-permute-done.5 = f32[32,512,64]{1,2,0:T(8,128)S(1)} collective-permute-done((f32[32,512,64]{1,2,0:T(8,128)S(1)}, f32[32,512,64]{1,2,0:T(8,128)S(1)}, u32[]{:S(2)}, u32[]{:S(2)}) %collective-permute-start.5) | collective-permute-done | bytes 4194336 | tf_op jit(solution)/shard_map/ppermute | solution.py:75
  1418.7 62.6 %all-reduce.10.cloned.1.call-done = f32[8192,64]{0,1:T(8,128)} async-done(((f32[8192,64]{0,1:T(8,128)}), f32[8192,64]{0,1:T(8,128)}) %all-reduce.10.cloned.1.call-update) | async-done | bytes 2097168 | tf_op jit(solution)/shard_map/psum | solution.py:87
  1487.8 8.8 all-gather.11.cloned.1.call-done
  1507.9 91.9 %all-reduce.12.cloned.1.call-done = (f32[128,128]{0,1:T(8,128)}, f32[1,128,128]{2,1,0:T(8,128)}, f32[1,128,128]{2,1,0:T(8,128)}) async-done(((f32[128,128]{0,1:T(8,128)}, f32[1,128,128]{2,1,0:T(8,128)}, f32[1,128,128]{2,1,0:T(8,128)}), (f32[128,128]{0,1:T(8,128)}, f32[1,128,128]{2,1,0:T(8,128)}, f32[1,128,128]{2,1,0:T(8,128)})) %all-reduce.12.cloned.1.call-update) | async-done | bytes 196624 | tf_op jit(solution)/shard_map/psum | solution.py:94
  1601.5 11.7 cholesky.55
  1614.6 9.8 custom-call.7
  (113 shorter events, 107.5 us)
Async XLA Ops:
  7.2 130.6 %all-gather.5.cloned.1.call-start = ((), (), s32[]{:S(2)}) async-start(), calls=%async_computation.2 | async-start | bytes 9437184 | tf_op jit(solution)/shard_map/all_gather | solution.py:52
  7.9 340.0 %reduce-scatter.3.cloned.1.call-start = ((), (), s32[]{:S(2)}) async-start(), calls=%async_computation.3 | async-start | bytes 9437184 | tf_op jit(solution)/shard_map/reduce_scatter | solution.py:70
  142.9 4.3 copy-start.10
  142.9 4.3 copy-start.11
  161.0 517.6 %all-reduce.6.cloned.1.call-start = ((), (), s32[]{:S(2)}) async-start(), calls=%async_computation.4 | async-start | bytes 4194304 | tf_op jit(solution)/shard_map/psum | solution.py:87
  347.9 25.2 %collective-permute-start = (f32[32,128,64]{1,2,0:T(8,128)}, f32[32,128,64]{1,2,0:T(8,128)S(1)}, u32[]{:S(2)}, u32[]{:S(2)}) collective-permute-start(f32[32,128,64]{1,2,0:T(8,128)} %reduce-scatter.3.cloned.1.call-done), channel_id=1, source_target_pairs={{0,4},{4,0},{8,12},{12,8},{16,20},{20,16},{24,28},{28,24},{1,5},{5... | collective-permute-start | bytes 3145736 | tf_op jit(solution)/shard_map/ppermute | solution.py:75
  376.3 46.9 %collective-permute-start.1 = (f32[32,256,64]{1,2,0:T(8,128)}, f32[32,256,64]{1,2,0:T(8,128)}, u32[]{:S(2)}, u32[]{:S(2)}) collective-permute-start(f32[32,256,64]{1,2,0:T(8,128)} %maximum_select_fusion.2), channel_id=1, source_target_pairs={{0,8},{4,12},{8,0},{12,4},{16,24},{20,28},{24,16},{28,20},{1,9},{5... | collective-permute-start | bytes 6291464 | tf_op jit(solution)/shard_map/ppermute | solution.py:75
  429.7 181.7 %collective-permute-start.2 = (f32[32,512,64]{1,2,0:T(8,128)}, f32[32,512,64]{1,2,0:T(8,128)}, u32[]{:S(2)}, u32[]{:S(2)}) collective-permute-start(f32[32,512,64]{1,2,0:T(8,128)} %maximum_select_fusion), channel_id=1, source_target_pairs={{0,16},{4,20},{8,24},{12,28},{16,0},{20,4},{24,8},{28,12},{1,17},{... | collective-permute-start | bytes 12582920 | tf_op jit(solution)/shard_map/ppermute | solution.py:75
  615.8 77.9 %all-gather.7.cloned.1.call-start = ((), (), s32[]{:S(2)}) async-start(), calls=%async_computation.5 | async-start | bytes 6291456 | tf_op jit(solution)/shard_map/all_gather | solution.py:90
  678.6 108.0 %all-reduce.8.cloned.1.call-start = ((), (), s32[]{:S(2)}) async-start(), calls=%async_computation.6 | async-start | bytes 131072 | tf_op jit(solution)/shard_map/psum | solution.py:94
  700.7 245.6 %all-gather.9.cloned.1.call-start = ((), (), s32[]{:S(2)}) async-start(), calls=%async_computation.7 | async-start | bytes 9437184 | tf_op jit(solution)/shard_map/all_gather | solution.py:52
  819.6 340.9 %reduce-scatter.5.cloned.1.call-start = ((), (), s32[]{:S(2)}) async-start(), calls=%async_computation.8 | async-start | bytes 9437184 | tf_op jit(solution)/shard_map/reduce_scatter | solution.py:70
  970.5 510.8 %all-reduce.10.cloned.1.call-start = ((), (), s32[]{:S(2)}) async-start(), calls=%async_computation.9 | async-start | bytes 4194304 | tf_op jit(solution)/shard_map/psum | solution.py:87
  1160.4 25.2 %collective-permute-start.3 = (f32[32,128,64]{1,2,0:T(8,128)}, f32[32,128,64]{1,2,0:T(8,128)S(1)}, u32[]{:S(2)}, u32[]{:S(2)}) collective-permute-start(f32[32,128,64]{1,2,0:T(8,128)} %reduce-scatter.5.cloned.1.call-done), channel_id=1, source_target_pairs={{0,4},{4,0},{8,12},{12,8},{16,20},{20,16},{24,28},{28,24},{1,5},{5... | collective-permute-start | bytes 3145736 | tf_op jit(solution)/shard_map/ppermute | solution.py:75
  1187.5 46.6 %collective-permute-start.4 = (f32[32,256,64]{1,2,0:T(8,128)S(1)}, f32[32,256,64]{1,2,0:T(8,128)S(1)}, u32[]{:S(2)}, u32[]{:S(2)}) collective-permute-start(f32[32,256,64]{1,2,0:T(8,128)S(1)} %maximum_select_fusion.3), channel_id=1, source_target_pairs={{0,8},{4,12},{8,0},{12,4},{16,24},{20,28},{24,16},{28,20},{1,9},{5... | collective-permute-start | bytes 6291464 | tf_op jit(solution)/shard_map/ppermute | solution.py:75
  1234.9 181.4 %collective-permute-start.5 = (f32[32,512,64]{1,2,0:T(8,128)S(1)}, f32[32,512,64]{1,2,0:T(8,128)S(1)}, u32[]{:S(2)}, u32[]{:S(2)}) collective-permute-start(f32[32,512,64]{1,2,0:T(8,128)S(1)} %maximum_select_fusion.1), channel_id=1, source_target_pairs={{0,16},{4,20},{8,24},{12,28},{16,0},{20,4},{24,8},{28,12},{1,17},{... | collective-permute-start | bytes 12582920 | tf_op jit(solution)/shard_map/ppermute | solution.py:75
  1417.0 64.4 %copy-start.3 = (bf16[8,1024,64]{1,2,0:T(8,128)(2,1)S(1)}, bf16[8,1024,64]{1,2,0:T(8,128)(2,1)}, u32[]{:S(2)}) copy-start(bf16[8,1024,64]{1,2,0:T(8,128)(2,1)} %get-tuple-element.499) | copy-start | bytes 3145732
  1418.7 78.0 %all-gather.11.cloned.1.call-start = ((), (), s32[]{:S(2)}) async-start(), calls=%async_computation.10 | async-start | bytes 6291456 | tf_op jit(solution)/shard_map/all_gather | solution.py:90
  1481.3 118.4 %all-reduce.12.cloned.1.call-start = ((), (), s32[]{:S(2)}) async-start(), calls=%async_computation.11 | async-start | bytes 393216 | tf_op jit(solution)/shard_map/psum | solution.py:94
  1486.2 20.5 %copy-start.4 = (f32[1,128,128]{2,1,0:T(8,128)}, f32[1,128,128]{2,1,0:T(8,128)S(1)}, u32[]{:S(2)}) copy-start(f32[1,128,128]{2,1,0:T(8,128)S(1)} %fusion.89) | copy-start | bytes 196612
  1486.3 15.0 copy-start.2
  1630.0 3.7 copy-start.1
  1630.0 3.0 copy-start.8
  1630.0 3.0 copy-start.9
  (4 other events, 4.2 us)
Sparse Core Ops, SparseCore 0:
  10.1 127.6 all-gather.4
  161.2 186.7 reduce-scatter.2
  616.0 62.5 all-reduce.5
  680.0 13.6 all-gather.6
  700.8 85.7 all-reduce.7
  819.7 126.5 all-gather.8
  970.6 189.7 reduce-scatter.4
  1418.8 62.4 all-reduce.9
  1482.9 13.6 all-gather.10
  1508.0 91.6 all-reduce.11
